TPU v7x, 256 devices: a whole 4x4x8 slice. The times are simulated.
256 devices in a mesh: tiles: 64 (over y, x, z_lo, core), season: 4 (over z_hi).
Axes of the slice: x: 4, y: 4, z: 8 (z_hi: 4, z_lo: 2; z = z_hi * 2 + z_lo), core: 2. Of those that a mesh axis runs over, the one named last changes fastest.
Arguments:
- yields: float32 [32, 3072, 2048], P('season', 'tiles'), may hold values from -6 to 6
- quality: float32 [32, 3072, 2048], P('season', 'tiles'), may hold values from 0.1 to 1
Outputs:
- anomalies: float32 [32, 3072, 2048], P('season', 'tiles')
- location: float32 [3072, 2048], P('tiles', 'season')
All inputs are finite; a program needn't handle non-finite values.
Results may differ from a plain program's by a relative error of at most 0.0001.
Values sent between devices are 32-bit elements; how exact they have to be, the bound alone decides.
A program may use at most 128 MiB of HBM per device.

v0:
```python
import jax
import jax.numpy as jnp
from jax import lax
from jax.sharding import PartitionSpec as P

PASSES = 4


window_reach = 15


def extended_2(block, sides, width):
    for axis, dim in sides:
        count = lax.axis_size(axis)
        forward = [(i, i + 1) for i in range(count - 1)]
        backward = [(target, source) for source, target in forward]
        low = lax.ppermute(
            lax.slice_in_dim(block, block.shape[dim] - width, None, axis=dim), axis, forward
        )
        high = lax.ppermute(lax.slice_in_dim(block, 0, width, axis=dim), axis, backward)
        block = jnp.concatenate([low, block, high], axis=dim)
    return block


def band(n_in, n_out):
    upper = lax.broadcasted_iota(jnp.int32, (n_in, n_out), 0)
    lower = lax.broadcasted_iota(jnp.int32, (n_in, n_out), 1)
    offset = (upper - lower - window_reach).astype(jnp.float32)
    taps = jnp.exp(-offset * offset / 128.0)
    return jnp.where(jnp.abs(offset) <= window_reach, taps, 0.0)


def smooth_columns(fields):
    cols_all = fields.shape[-1]
    width = min(cols_all, 256)
    padded = jnp.pad(fields, [(0, 0)] * (fields.ndim - 1) + [(window_reach, window_reach)])
    kernel = band(width + 2 * window_reach, width)
    pieces = []
    for block in range(cols_all // width):
        window = padded[..., block * width : block * width + width + 2 * window_reach]
        pieces.append(jnp.einsum("fsrk,kj->fsrj", window, kernel, precision=lax.Precision.HIGHEST))
    return jnp.concatenate(pieces, axis=-1)


def tukey(field, count, first, spread_sum, weighted):
    loc = first(jnp.sum(field, axis=0)) / count
    for step in range(PASSES):
        resid = field - loc
        spread = jnp.sqrt(spread_sum(jnp.sum(resid * resid, axis=0)) / count + 1.0)
        ratio = resid / (1.5 * spread)
        weight = jnp.square(jnp.maximum(1.0 - ratio * ratio, 0.0))
        upper, lower = weighted(jnp.sum(weight * resid, axis=0), jnp.sum(weight, axis=0))
        loc = loc + upper / (lower + 1.0)
    return (loc, field - loc)


def keep(value):
    return value


def keep_pair(first_val, second_val):
    return (first_val, second_val)


def on_device(yields, quality):
    row_own = yields.shape[1]
    stacked = jnp.stack([yields, quality])
    extended = extended_2(stacked, (("tiles", 2),), 15)
    value, weight = (extended[0], extended[1])
    fields = jnp.stack([weight * value, weight * value * value, weight])
    rowwise = jnp.einsum(
        "fsjc,ji->fsic",
        fields,
        band(row_own + 2 * window_reach, row_own),
        precision=lax.Precision.HIGHEST,
    )
    filtered = smooth_columns(rowwise)
    mean = filtered[0] / filtered[2]
    second = filtered[1] / filtered[2]
    field = (yields - mean) / jnp.sqrt(second - mean * mean + 0.1)
    groups = lax.axis_size("season")
    count = field.shape[0] * groups
    cells = lax.all_to_all(field, "season", split_axis=2, concat_axis=0, tiled=True)
    loc, resid = tukey(cells, count, keep, keep, keep_pair)
    anomalies = lax.all_to_all(resid, "season", split_axis=0, concat_axis=2, tiled=True)
    return (anomalies, loc)


def solution(mesh):
    placed = (P("season", "tiles", None), P("season", "tiles", None))
    return jax.shard_map(
        on_device,
        mesh=mesh,
        in_specs=placed,
        out_specs=(P("season", "tiles", None), P("tiles", "season")),
        check_vma=False,
    )
```

profile of v0, /device:TPU:10, one launch (start us, length us, event | category | flops | bytes accessed | tf_op | source)
XLA Modules:
  0.0 330.7 jit_solution(4396434335882955082)
XLA Ops:
  0.6 2.6 pad_maximum_fusion.2
  3.2 1.1 copy.13
  4.4 1.9 collective-permute-start
  6.3 1.1 copy.14
  7.4 0.0 copy-start
  7.5 5.1 %collective-permute-start.1 = (f32[2,8,15,2048]{3,1,2,0:T(8,128)S(1)}, f32[2,8,15,2048]{3,1,2,0:T(8,128)S(1)}, u32[]{:S(2)}, u32[]{:S(2)}) collective-permute-start(f32[2,8,15,2048]{3,1,2,0:T(8,128)S(1)} %copy.14), channel_id=1, source_target_pairs={{4,0},{8,4},{12,8},{16,12},{20,16},{24,20},{28,24},{32,28},{36,32}... | collective-permute-start | bytes 5898248 | tf_op jit(solution)/shard_map/ppermute | solution.py:20
  12.6 35.0 %collective-permute-done = f32[2,8,15,2048]{3,1,2,0:T(8,128)S(1)} collective-permute-done((f32[2,8,15,2048]{3,1,2,0:T(8,128)S(1)}, f32[2,8,15,2048]{3,1,2,0:T(8,128)S(1)}, u32[]{:S(2)}, u32[]{:S(2)}) %collective-permute-start) | collective-permute-done | bytes 1966112 | tf_op jit(solution)/shard_map/ppermute | solution.py:17
  47.6 2.4 copy.15
  50.0 0.8 collective-permute-done.1
  50.8 2.5 copy.16
  53.3 0.0 copy-done
  53.3 9.1 %pad_maximum_fusion = f32[2,8,78,2048]{3,2,1,0:T(8,128)} fusion(f32[2,8,15,2048]{3,2,1,0:T(8,128)} %copy.16, f32[1,8,48,2048]{3,2,1,0:T(8,128)} %bitcast.81, f32[1,8,48,2048]{3,2,1,0:T(8,128)S(1)} %bitcast.79, f32[2,8,15,2048]{3,2,1,0:T(8,128)} %copy.15), kind=kLoop, calls=%fused_computation.6 | loop fusion | flops 7667712 | bytes 20447232 | tf_op jit(solution)/shard_map/concatenate | solution.py:21
  62.4 12.2 %slice_multiply_fusion = (f32[1,8,78,2048]{3,2,1,0:T(8,128)}, f32[1,8,78,2048]{3,2,1,0:T(8,128)}, f32[1,8,78,2048]{3,2,1,0:T(8,128)}) fusion(f32[2,8,78,2048]{3,2,1,0:T(8,128)} %pad_maximum_fusion), kind=kLoop, calls=%fused_computation.9 | loop fusion | flops 2555904 | bytes 25559040 | tf_op jit(solution)/shard_map/mul | solution.py:70
  74.5 14.2 %fusion.6 = f32[3,8,48,2048]{3,2,1,0:T(8,128)S(1)} fusion(f32[1,8,78,2048]{3,2,1,0:T(8,128)} %get-tuple-element.12, f32[1,8,78,2048]{3,2,1,0:T(8,128)} %get-tuple-element.10, f32[1,8,78,2048]{3,2,1,0:T(8,128)} %get-tuple-element.11), kind=kOutput, calls=%fused_computation.11 | convolution fusion | flops 2216002560 | bytes 24772608 | tf_op jit(solution)/shard_map/fsjc,ji->fsic/dot_general | solution.py:71
  88.7 2.3 fusion.42
  91.0 2.2 fusion.43
  93.3 2.3 fusion.46
  95.5 2.2 fusion.49
  97.8 2.2 fusion.52
  100.0 2.4 fusion.55
  102.5 2.3 fusion.58
  104.8 2.2 fusion.41
  107.0 2.6 fusion.25
  109.6 6.7 %copy.17 = f32[8,48,2048]{1,0,2:T(8,128)} copy(f32[8,48,2048]{2,1,0:T(8,128)} %fusion.25) | data formatting | bytes 6291456 | tf_op jit(solution)/shard_map/div | solution.py:80
  116.3 10.2 %reshape.95 = f32[4,1,196608]{2,1,0:T(1,128)} reshape(f32[2048,8,48]{2,1,0:T(8,128)} %bitcast.76) | data formatting | bytes 6291456
  126.5 83.2 %all_to_all.36 = f32[4,1,196608]{2,1,0:T(1,128)S(1)} all-to-all(f32[4,1,196608]{2,1,0:T(1,128)} %reshape.95), channel_id=1, replica_groups=mesh['tiles'=64,'season'=4] {'season'}, dimensions={0} | all-to-all | bytes 6291456 | tf_op jit(solution)/shard_map/all_to_all | solution.py:83
  209.7 0.5 broadcast.266
  210.2 10.6 %reduce.13 = f32[4,196608]{1,0:T(4,128)} reduce(f32[4,1,196608]{2,1,0:T(1,128)S(1)} %all_to_all.36, f32[]{:T(128)} %broadcast.266), dimensions={1}, to_apply=%all_to_all.26.reduce_sub_computation | reduce | bytes 6291460 | tf_op jit(solution)/shard_map/all_to_all | solution.py:83
  220.8 9.0 %reshape.96 = f32[2048,8,48]{2,1,0:T(8,128)} reshape(f32[4,196608]{1,0:T(4,128)} %reduce.13) | data formatting | bytes 6291456
  229.8 5.4 %copy.23 = f32[8,48,4,512]{3,2,1,0:T(4,128)S(1)} copy(f32[8,48,4,512]{1,0,3,2:T(8,128)} %bitcast.77) | data formatting | bytes 6291456 | tf_op jit(solution)/shard_map/all_to_all | solution.py:83
  235.2 0.6 bitcast_reduce_fusion
  235.8 1.0 multiply_reduce_fusion.7
  236.9 2.7 fusion.159
  239.6 1.0 multiply_reduce_fusion.5
  240.7 3.0 fusion.158
  243.7 1.0 multiply_reduce_fusion.3
  244.7 2.7 fusion.157
  247.4 1.0 multiply_reduce_fusion.1
  248.5 2.7 fusion.156
  251.2 1.0 copy.19
  252.3 0.0 copy-start.1
  252.3 0.6 bitcast_subtract_fusion
  252.8 0.1 copy-done.1
  252.9 75.5 %all_to_all.37 = f32[32,48,512]{2,1,0:T(8,128)S(1)} all-to-all(f32[32,48,512]{2,1,0:T(8,128)S(1)} %bitcast_subtract_fusion), channel_id=1, replica_groups=mesh['tiles'=64,'season'=4] {'season'}, dimensions={0} | all-to-all | bytes 6291456 | tf_op jit(solution)/shard_map/all_to_all | solution.py:85
  328.5 2.0 copy.24
  (9 shorter events, 0.3 us)
Async XLA Ops:
  4.4 43.2 %collective-permute-start = (f32[2,8,15,2048]{3,1,2,0:T(8,128)S(1)}, f32[2,8,15,2048]{3,1,2,0:T(8,128)S(1)}, u32[]{:S(2)}, u32[]{:S(2)}) collective-permute-start(f32[2,8,15,2048]{3,1,2,0:T(8,128)S(1)} %copy.13), channel_id=1, source_target_pairs={{0,4},{4,8},{8,12},{12,16},{16,20},{20,24},{24,28},{28,32},{32,36}... | collective-permute-start | bytes 5898248 | tf_op jit(solution)/shard_map/ppermute | solution.py:17
  7.4 45.8 %copy-start = (f32[8,48,2048]{2,1,0:T(8,128)S(1)}, f32[8,48,2048]{2,1,0:T(8,128)}, u32[]{:S(2)}) copy-start(f32[8,48,2048]{2,1,0:T(8,128)} %param.2) | copy-start | bytes 9437188
  7.5 43.4 %collective-permute-start.1 = (f32[2,8,15,2048]{3,1,2,0:T(8,128)S(1)}, f32[2,8,15,2048]{3,1,2,0:T(8,128)S(1)}, u32[]{:S(2)}, u32[]{:S(2)}) collective-permute-start(f32[2,8,15,2048]{3,1,2,0:T(8,128)S(1)} %copy.14), channel_id=1, source_target_pairs={{4,0},{8,4},{12,8},{16,12},{20,16},{24,20},{28,24},{32,28},{36,32}... | collective-permute-start | bytes 5898248 | tf_op jit(solution)/shard_map/ppermute | solution.py:20
  252.3 0.7 copy-start.1
where the time goes:
time: 334 us; the launch traced here: 331 us
  blocking collectives  159 us (48%)
  other arithmetic  53.5 us (16%)
  local copies, waits for them, and re-layouts  42.1 us (13%)
  waiting for transfers between devices  35.8 us (11%)
  matrix products  32.4 us (10%)
  starting transfers between devices  7.02 us (2%)
    all_to_all x1, blocking collectives, on_device(): lax.all_to_all(field, 'season', split_axis=2, concat_axis=0, tiled=True)  83.2 us
    all_to_all x1, blocking collectives, on_device(): lax.all_to_all(resid, 'season', split_axis=0, concat_axis=2, tiled=True)  75.5 us
    ppermute x1, waiting for transfers between devices, extended_2(): lax.ppermute(lax.slice_in_dim(block, block.shape[dim] - width, None, axis...  35 us
    unnamed x6, local copies, waits for them, and re-layouts  19.3 us
    dot_general x8, matrix products, smooth_columns(): jnp.einsum('fsrk,kj->fsrj', window, kernel, precision=lax.Precision.HIGHEST)  18.2 us
    dot_general x1, matrix products, on_device(): jnp.einsum('fsjc,ji->fsic', fields, band(row_own + 2 * window_reach, row_...  14.2 us
    mul x1, other arithmetic, on_device(): fields = jnp.stack([weight * value, weight * value * value, weight])  12.2 us
    reduce_sum x4, other arithmetic, tukey(): jnp.sum(weight, axis=0)  11.1 us
  transfers between devices with their start and end apart: 2, of which 2 were waited for; matrix products, arithmetic and copies ran while one was open for 1% of the time, Pallas kernels for 0%

commit v1 on v0

v1 whole, which is shorter than its diff:
```python
import functools

import jax
import jax.numpy as jnp
from jax import lax
from jax.experimental import pallas as pl
from jax.experimental.pallas import tpu as pltpu
from jax.sharding import PartitionSpec as P

MESH = pl.DeviceIdType.MESH
PASSES = 4
REACH = 15
F32 = jnp.float32
BF16 = jnp.bfloat16

GROUP = 16
WINDOW = GROUP + 32
WIDTH = 256
SPAN = WIDTH + 256
CHUNK = 512


def tap(offset):
    value = offset.astype(F32)
    return jnp.where(jnp.abs(value) <= REACH, jnp.exp(-value * value / 128.0), 0.0)


def halves(value):
    high = value.astype(BF16)
    return high, (value - high.astype(F32)).astype(BF16)


def kernel(
    tiles, groups, y_ref, q_ref, z_out, loc_out, own_out,
    yext, qext, rowwise, zbuf, cells, loc, row_band, col_high, col_low,
    own_sem, near_send, near_recv, far_send, far_recv,
    z_send, z_recv, z_local, loc_send, loc_recv, out_sem,
):
    tile = lax.axis_index("tiles")
    home = lax.axis_index("season")
    core = lax.rem(tile, 2)
    seasons, rows, cols = y_ref.shape
    block = cols // groups
    subs = block // WIDTH

    near = tile + 1 - 2 * core
    far = lax.rem(tile + 2 * core - 1 + tiles, tiles)

    loads = []
    for i, (src, dst) in enumerate(((y_ref, yext), (q_ref, qext))):
        copy = pltpu.make_async_copy(src, dst.at[:, pl.ds(GROUP, rows), :], own_sem.at[i])
        copy.start()
        loads.append(copy)

    barrier = pltpu.get_barrier_semaphore()
    partners = [(near, home), (far, home)]
    partners += [(tile, lax.rem(home + d, groups)) for d in range(1, groups)]
    for partner in partners:
        pl.semaphore_signal(barrier, inc=1, device_id=partner, device_id_type=MESH)
    pl.semaphore_wait(barrier, len(partners))

    def halo(partner, src_row, dst_row, send, recv):
        copies = []
        for i, (src, dst) in enumerate(((y_ref, yext), (q_ref, qext))):
            copies.append(
                pltpu.make_async_remote_copy(
                    src_ref=src.at[:, pl.ds(pl.multiple_of(src_row, GROUP), GROUP), :],
                    dst_ref=dst.at[:, pl.ds(pl.multiple_of(dst_row, GROUP), GROUP), :],
                    send_sem=send.at[i],
                    recv_sem=recv.at[i],
                    device_id=(partner, home),
                    device_id_type=MESH,
                )
            )
        return copies

    top, bottom = 0, rows - GROUP
    past = rows + GROUP
    far_copies = halo(far, bottom * core, past * (1 - core), far_send, far_recv)
    for copy in far_copies:
        copy.start()
    near_copies = halo(near, bottom * (1 - core), past * core, near_send, near_recv)
    for copy in near_copies:
        copy.start()

    out_row = lax.broadcasted_iota(jnp.int32, (3 * GROUP, 3 * WINDOW), 0)
    in_row = lax.broadcasted_iota(jnp.int32, (3 * GROUP, 3 * WINDOW), 1)
    same = out_row // GROUP == in_row // WINDOW
    offset = lax.rem(in_row, WINDOW) - GROUP - lax.rem(out_row, GROUP)
    high, low = halves(jnp.where(same, tap(offset), 0.0))
    row_band[pl.ds(0, 3 * GROUP), :] = high
    row_band[pl.ds(3 * GROUP, 3 * GROUP), :] = low
    in_col = lax.broadcasted_iota(jnp.int32, (SPAN, WIDTH), 0)
    out_col = lax.broadcasted_iota(jnp.int32, (SPAN, WIDTH), 1)
    high, low = halves(tap(in_col - 128 - out_col))
    col_high[...] = high
    col_low[...] = low
    count = 3 * GROUP * seasons
    edge = jnp.zeros((2 * count, 128), BF16)
    rowwise[:, pl.ds(0, 128)] = edge
    rowwise[:, pl.ds(cols + 128, 128)] = edge

    for copy in loads:
        copy.wait()

    def z_copy(g, n, row0, local=False):
        sub, d = n // groups, lax.rem(n + 1, groups)
        to = lax.rem(home + d, groups)
        src = zbuf.at[
            :,
            pl.ds(pl.multiple_of(row0, GROUP), GROUP),
            pl.ds(pl.multiple_of(to * block + sub * WIDTH, WIDTH), WIDTH),
        ]
        dst = cells.at[
            home,
            :,
            pl.ds(pl.multiple_of(row0, GROUP), GROUP),
            pl.ds(pl.multiple_of(sub * WIDTH, WIDTH), WIDTH),
        ]
        if local:
            return pltpu.make_async_copy(src, dst, z_local.at[g, sub])
        return pltpu.make_async_remote_copy(
            src_ref=src,
            dst_ref=dst,
            send_sem=z_send.at[g, n],
            recv_sem=z_recv.at[g, n],
            device_id=(tile, to),
            device_id_type=MESH,
        )

    def smooth(g, row0):
        def row_step(n, carry):
            s, c = n // (cols // CHUNK), lax.rem(n, cols // CHUNK)
            at = (s, pl.ds(pl.multiple_of(row0, GROUP), WINDOW), pl.ds(pl.multiple_of(c * CHUNK, CHUNK), CHUNK))
            value, weight = yext[at], qext[at]
            first = weight * value
            high, low = halves(jnp.concatenate([first, first * value, weight], axis=0))
            both = jnp.dot(row_band[...], high, preferred_element_type=F32)
            rest = jnp.dot(row_band[pl.ds(0, 3 * GROUP), :], low, preferred_element_type=F32)
            high, low = halves(both[: 3 * GROUP] + both[3 * GROUP :] + rest)
            for f in range(3):
                for part, base in ((high, 0), (low, count)):
                    rowwise[
                        pl.ds(pl.multiple_of(base + f * seasons * GROUP + s * GROUP, GROUP), GROUP),
                        pl.ds(pl.multiple_of(c * CHUNK + 128, 128), CHUNK),
                    ] = part[f * GROUP : (f + 1) * GROUP]
            return carry

        lax.fori_loop(0, seasons * (cols // CHUNK), row_step, 0)

        def col_step(n, carry):
            d = lax.rem(n + 1, groups)
            col0 = lax.rem(home + d, groups) * block + (n // groups) * WIDTH
            window = rowwise[:, pl.ds(pl.multiple_of(col0, WIDTH), SPAN)]
            both = jnp.dot(window, col_high[...], preferred_element_type=F32)
            rest = jnp.dot(window[:count], col_low[...], preferred_element_type=F32)
            fields = both[:count] + both[count:] + rest
            fields = fields.reshape(3, seasons, GROUP, WIDTH)
            total = 1.0 / fields[2]
            mean = fields[0] * total
            second = fields[1] * total
            here = pl.ds(pl.multiple_of(col0, WIDTH), WIDTH)
            value = yext[:, pl.ds(pl.multiple_of(row0 + GROUP, GROUP), GROUP), here]
            zbuf[:, pl.ds(pl.multiple_of(row0, GROUP), GROUP), here] = (value - mean) * lax.rsqrt(
                second - mean * mean + 0.1
            )

            @pl.when(d != 0)
            def _():
                z_copy(g, n, row0).start()

            @pl.when(d == 0)
            def _():
                z_copy(g, n, row0, local=True).start()

            return carry

        lax.fori_loop(0, subs * groups, col_step, 0)
        copy = pltpu.make_async_copy(
            zbuf.at[:, pl.ds(pl.multiple_of(row0, GROUP), GROUP), :],
            z_out.at[:, pl.ds(pl.multiple_of(row0, GROUP), GROUP), :],
            out_sem.at[g],
        )
        copy.start()
        return copy

    def clear(dst_row):
        qext[:, pl.ds(dst_row, GROUP), :] = jnp.zeros((seasons, GROUP, cols), F32)

    where = [GROUP, bottom * (1 - core), bottom * core]
    outs = [smooth(0, where[0])]
    for copy in near_copies:
        copy.wait_recv()
    outs.append(smooth(1, where[1]))
    for copy in far_copies:
        copy.wait_recv()

    @pl.when(tile == 0)
    def _():
        clear(0)

    @pl.when(tile == tiles - 1)
    def _():
        clear(past)

    outs.append(smooth(2, where[2]))

    def loc_copies(g, sub, row0):
        part = loc.at[
            pl.ds(pl.multiple_of(row0, GROUP), GROUP),
            pl.ds(pl.multiple_of(home * block + sub * WIDTH, WIDTH), WIDTH),
        ]
        return [
            pltpu.make_async_remote_copy(
                src_ref=part,
                dst_ref=part,
                send_sem=loc_send.at[g, sub, d - 1],
                recv_sem=loc_recv.at[g, sub, d - 1],
                device_id=(tile, lax.rem(home + d, groups)),
                device_id_type=MESH,
            )
            for d in range(1, groups)
        ]

    def tukey(g, sub, row0):
        for n in range(sub * groups, (sub + 1) * groups):
            if (n + 1) % groups:
                z_copy(g, n, row0).wait_recv()
            else:
                z_copy(g, n, row0, local=True).wait()

        def cell_step(n, carry):
            r = row0 + 8 * (n // (WIDTH // 128))
            c = sub * WIDTH + 128 * lax.rem(n, WIDTH // 128)
            field = cells[:, :, pl.ds(pl.multiple_of(r, 8), 8), pl.ds(pl.multiple_of(c, 128), 128)]
            field = field.reshape(groups * seasons, 8, 128)
            number = groups * seasons
            centre = jnp.sum(field, axis=0) / number
            for _ in range(PASSES):
                resid = field - centre
                square = resid * resid
                spread = 2.25 * (jnp.sum(square, axis=0) / number + 1.0)
                root = jnp.maximum(1.0 - square * (1.0 / spread), 0.0)
                weight = root * root
                centre = centre + jnp.sum(weight * resid, axis=0) / (jnp.sum(weight, axis=0) + 1.0)
            loc[pl.ds(pl.multiple_of(r, 8), 8), pl.ds(pl.multiple_of(home * block + c, 128), 128)] = centre
            return carry

        lax.fori_loop(0, (GROUP // 8) * (WIDTH // 128), cell_step, 0)
        for copy in loc_copies(g, sub, row0):
            copy.start()

    for g in range(3):
        for sub in range(subs):
            tukey(g, sub, where[g])
    own = pltpu.make_async_copy(
        loc.at[:, pl.ds(pl.multiple_of(home * block, block), block)], own_out, out_sem.at[3]
    )
    own.start()
    for g in range(3):
        for sub in range(subs):
            for copy in loc_copies(g, sub, where[g]):
                copy.wait_recv()
    whole = pltpu.make_async_copy(loc, loc_out, out_sem.at[4])
    whole.start()

    for copy in near_copies + far_copies:
        copy.wait_send()
    for g in range(3):
        for n in range(subs * groups):
            if (n + 1) % groups:
                z_copy(g, n, where[g]).wait_send()
        for sub in range(subs):
            for copy in loc_copies(g, sub, where[g]):
                copy.wait_send()
    for copy in outs + [own, whole]:
        copy.wait()


def on_device(yields, quality):
    seasons, rows, cols = yields.shape
    tiles, groups = lax.axis_size("tiles"), lax.axis_size("season")
    block = cols // groups
    subs = block // WIDTH
    dma = pltpu.SemaphoreType.DMA
    anywhere = pl.BlockSpec(memory_space=pl.ANY)
    field, loc, own = pl.pallas_call(
        functools.partial(kernel, tiles, groups),
        out_shape=(
            jax.ShapeDtypeStruct((seasons, rows, cols), F32),
            jax.ShapeDtypeStruct((rows, cols), F32),
            jax.ShapeDtypeStruct((rows, block), F32),
        ),
        in_specs=[anywhere] * 2,
        out_specs=(anywhere,) * 3,
        scratch_shapes=[
            pltpu.VMEM((seasons, rows + 2 * GROUP, cols), F32),
            pltpu.VMEM((seasons, rows + 2 * GROUP, cols), F32),
            pltpu.VMEM((6 * GROUP * seasons, cols + 256), BF16),
            pltpu.VMEM((seasons, rows, cols), F32),
            pltpu.VMEM((groups, seasons, rows, block), F32),
            pltpu.VMEM((rows, cols), F32),
            pltpu.VMEM((6 * GROUP, 3 * WINDOW), BF16),
            pltpu.VMEM((SPAN, WIDTH), BF16),
            pltpu.VMEM((SPAN, WIDTH), BF16),
            dma((2,)),
            dma((2,)),
            dma((2,)),
            dma((2,)),
            dma((2,)),
            dma((3, subs * groups)),
            dma((3, subs * groups)),
            dma((3, subs)),
            dma((3, subs, groups - 1)),
            dma((3, subs, groups - 1)),
            dma((5,)),
        ],
        compiler_params=pltpu.CompilerParams(
            collective_id=0, has_side_effects=True, vmem_limit_bytes=48 << 20
        ),
        name="field_and_location",
    )(yields, quality)
    return field - loc, own


def solution(mesh):
    placed = (P("season", "tiles", None), P("season", "tiles", None))
    return jax.shard_map(
        on_device,
        mesh=mesh,
        in_specs=placed,
        out_specs=(P("season", "tiles", None), P("tiles", "season")),
        check_vma=False,
    )
```

time: 334 us -> 138 us (0.41)
  blocking collectives: 159 us -> 0 us
  Pallas kernels: 0 us -> 134 us
  other arithmetic: 53.5 us -> 2.06 us
  local copies, waits for them, and re-layouts: 42.1 us -> 0.64 us
  waiting for transfers between devices: 35.8 us -> 0 us
  matrix products: 32.4 us -> 0 us
  starting transfers between devices: 7.02 us -> 0 us
    all_to_all x2 -> x0, blocking collectives: 159 us -> none  [the longest x1 83.2 us: on_device(): lax.all_to_all(field, 'season', split_axis=2, concat_axis=0, tiled=True)]
    pallas_call x0 -> x1, Pallas kernels: none -> 134 us  [on_device(): pl.pallas_call(functools.partial(kernel, tiles, groups), out_shape=(jax.S...]
    ppermute x2 -> x0, waiting for transfers between devices: 35.8 us -> none  [the longest x1 35 us: extended_2(): lax.ppermute(lax.slice_in_dim(block, block.shape[dim] - width, None, axis...]
    dot_general x9 -> x0, matrix products: 32.4 us -> none  [the longest x8 18.2 us: smooth_columns(): jnp.einsum('fsrk,kj->fsrj', window, kernel, precision=lax.Precision.HIGHEST)]
    unnamed x6 -> x1, local copies, waits for them, and re-layouts: 19.3 us -> 0.64 us
    reduce_sum x9 -> x0, other arithmetic: 15.6 us -> none  [the longest x4 11.1 us: tukey(): jnp.sum(weight, axis=0)]
    mul x5 -> x0, other arithmetic: 12.3 us -> none  [the longest x1 12.2 us: on_device(): fields = jnp.stack([weight * value, weight * value * value, weight])]
    all_to_all x1 -> x0, other arithmetic: 10.6 us -> none  [on_device(): lax.all_to_all(field, 'season', split_axis=2, concat_axis=0, tiled=True)]
  transfers between devices with their start and end apart: 2 -> 0, of which waited for: 2 -> 0; matrix products, arithmetic and copies ran while one was open for 1% -> 0% of each run, Pallas kernels for 0% -> 0%
where the time goes in v1:
time: 138 us; the launch traced here: 137 us
  Pallas kernels  134 us (97%)
  other arithmetic  2.06 us (1%)
    pallas_call x1, Pallas kernels, on_device(): pl.pallas_call(functools.partial(kernel, tiles, groups), out_shape=(jax.S...  134 us

profile of v1, /device:TPU:10, one launch (start us, length us, event | category | flops | bytes accessed | tf_op | source)
XLA Modules:
  0.0 137.4 jit_solution(1410109310561967781)
XLA Ops:
  0.6 134.1 %field_and_location.1 = (f32[8,48,2048]{2,1,0:T(8,128)S(1)}, f32[48,2048]{1,0:T(8,128)S(1)}, f32[48,512]{1,0:T(8,128)S(1)}) custom-call(f32[8,48,2048]{2,1,0:T(8,128)} %y_ref.1, f32[8,48,2048]{2,1,0:T(8,128)} %q_ref.1), custom_call_target="tpu_custom_call" | custom-call | tf_op jit(solution)/shard_map/field_and_location/pallas_call | solution.py:287
  134.7 2.1 %broadcast_subtract_fusion = f32[8,48,2048]{2,1,0:T(8,128)} fusion(f32[8,48,2048]{2,1,0:T(8,128)S(1)} %get-tuple-element.5, f32[48,2048]{1,0:T(8,128)S(1)} %get-tuple-element.6), kind=kLoop, calls=%fused_computation | loop fusion | flops 786432 | bytes 6684672 | tf_op jit(solution)/shard_map/sub | solution.py:323
  136.8 0.6 copy.5

commit v2 on v1

--- a/solution.py
+++ b/solution.py
@@ -16,6 +16,7 @@
 GROUP = 16
 WINDOW = GROUP + 32
 WIDTH = 256
+PART = 256
 SPAN = WIDTH + 256
 CHUNK = 512
 
@@ -32,8 +33,8 @@
 
 def kernel(
     tiles, groups, y_ref, q_ref, z_out, loc_out, own_out,
-    yext, qext, rowwise, zbuf, cells, loc, row_band, col_high, col_low,
-    own_sem, near_send, near_recv, far_send, far_recv,
+    yext, qext, packed, rowwise, zbuf, cells, loc, row_band, col_high, col_low,
+    own_sem, near_send, near_recv, far_send, far_recv, outer_send, outer_recv,
     z_send, z_recv, z_local, loc_send, loc_recv, out_sem,
 ):
     tile = lax.axis_index("tiles")
@@ -41,7 +42,7 @@
     core = lax.rem(tile, 2)
     seasons, rows, cols = y_ref.shape
     block = cols // groups
-    subs = block // WIDTH
+    subs = block // PART
 
     near = tile + 1 - 2 * core
     far = lax.rem(tile + 2 * core - 1 + tiles, tiles)
@@ -59,13 +60,13 @@
         pl.semaphore_signal(barrier, inc=1, device_id=partner, device_id_type=MESH)
     pl.semaphore_wait(barrier, len(partners))
 
-    def halo(partner, src_row, dst_row, send, recv):
+    def halo(partner, src_row, dst_row, count, send, recv):
         copies = []
         for i, (src, dst) in enumerate(((y_ref, yext), (q_ref, qext))):
             copies.append(
                 pltpu.make_async_remote_copy(
-                    src_ref=src.at[:, pl.ds(pl.multiple_of(src_row, GROUP), GROUP), :],
-                    dst_ref=dst.at[:, pl.ds(pl.multiple_of(dst_row, GROUP), GROUP), :],
+                    src_ref=src.at[:, pl.ds(pl.multiple_of(src_row, 8), count), :],
+                    dst_ref=dst.at[:, pl.ds(pl.multiple_of(dst_row, 8), count), :],
                     send_sem=send.at[i],
                     recv_sem=recv.at[i],
                     device_id=(partner, home),
@@ -74,14 +75,46 @@
             )
         return copies
 
-    top, bottom = 0, rows - GROUP
+    bottom = rows - GROUP
     past = rows + GROUP
-    far_copies = halo(far, bottom * core, past * (1 - core), far_send, far_recv)
+    far_copies = halo(far, (rows - 8) * core, past - (past - 8) * core, 8, far_send, far_recv)
     for copy in far_copies:
         copy.start()
-    near_copies = halo(near, bottom * (1 - core), past * core, near_send, near_recv)
+    near_copies = halo(near, bottom * (1 - core), past * core, GROUP, near_send, near_recv)
     for copy in near_copies:
         copy.start()
+    for copy in loads:
+        copy.wait()
+    line = lax.broadcasted_iota(jnp.int32, (8, cols), 0)
+    last = seasons - 1
+    spare = 7 * (1 - core)
+    outer_row = pl.ds(pl.multiple_of(GROUP + 8 + (rows - 24) * core, 8), 8)
+    outer_copies = []
+    for i, ext in enumerate((yext, qext)):
+        extra = ext[last, outer_row, :]
+        for s in range(last):
+            row = jnp.where(core == 0, extra[s : s + 1], extra[s + 1 : s + 2])
+            packed[i, s] = jnp.where(line == spare, row, ext[s, outer_row, :])
+        copy = pltpu.make_async_remote_copy(
+            src_ref=packed.at[i],
+            dst_ref=ext.at[pl.ds(0, last), pl.ds(pl.multiple_of((past + 8) * (1 - core), 8), 8), :],
+            send_sem=outer_send.at[i],
+            recv_sem=outer_recv.at[i],
+            device_id=(far, home),
+            device_id_type=MESH,
+        )
+        copy.start()
+        outer_copies.append(copy)
+
+    def unpack():
+        where_outer = pl.ds(pl.multiple_of((past + 8) * core, 8), 8)
+        for ext in (yext, qext):
+            tile_last = jnp.zeros((8, cols), F32)
+            for s in range(last):
+                held = ext[s, where_outer, :]
+                row = jnp.where(core == 0, held[0:1], held[7:8])
+                tile_last = jnp.where(line == s + 1 - core, row, tile_last)
+            ext[last, where_outer, :] = tile_last
 
     out_row = lax.broadcasted_iota(jnp.int32, (3 * GROUP, 3 * WINDOW), 0)
     in_row = lax.broadcasted_iota(jnp.int32, (3 * GROUP, 3 * WINDOW), 1)
@@ -100,22 +133,19 @@
     rowwise[:, pl.ds(0, 128)] = edge
     rowwise[:, pl.ds(cols + 128, 128)] = edge
 
-    for copy in loads:
-        copy.wait()
-
     def z_copy(g, n, row0, local=False):
         sub, d = n // groups, lax.rem(n + 1, groups)
         to = lax.rem(home + d, groups)
         src = zbuf.at[
             :,
             pl.ds(pl.multiple_of(row0, GROUP), GROUP),
-            pl.ds(pl.multiple_of(to * block + sub * WIDTH, WIDTH), WIDTH),
+            pl.ds(pl.multiple_of(to * block + sub * PART, PART), PART),
         ]
         dst = cells.at[
             home,
             :,
             pl.ds(pl.multiple_of(row0, GROUP), GROUP),
-            pl.ds(pl.multiple_of(sub * WIDTH, WIDTH), WIDTH),
+            pl.ds(pl.multiple_of(sub * PART, PART), PART),
         ]
         if local:
             return pltpu.make_async_copy(src, dst, z_local.at[g, sub])
@@ -165,17 +195,9 @@
                 second - mean * mean + 0.1
             )
 
-            @pl.when(d != 0)
-            def _():
-                z_copy(g, n, row0).start()
-
-            @pl.when(d == 0)
-            def _():
-                z_copy(g, n, row0, local=True).start()
-
             return carry
 
-        lax.fori_loop(0, subs * groups, col_step, 0)
+        lax.fori_loop(0, block // WIDTH * groups, col_step, 0)
         copy = pltpu.make_async_copy(
             zbuf.at[:, pl.ds(pl.multiple_of(row0, GROUP), GROUP), :],
             z_out.at[:, pl.ds(pl.multiple_of(row0, GROUP), GROUP), :],
@@ -188,12 +210,27 @@
         qext[:, pl.ds(dst_row, GROUP), :] = jnp.zeros((seasons, GROUP, cols), F32)
 
     where = [GROUP, bottom * (1 - core), bottom * core]
+    chunks = [(g, sub) for g in range(3) for sub in range(subs)]
+
+    def send(g, sub):
+        def send_step(d, carry):
+            z_copy(g, sub * groups + d - 1, where[g]).start()
+            return carry
+
+        z_copy(g, sub * groups + groups - 1, where[g], local=True).start()
+        lax.fori_loop(1, groups, send_step, 0)
+
     outs = [smooth(0, where[0])]
+    for sub in range(subs):
+        send(0, sub)
     for copy in near_copies:
         copy.wait_recv()
     outs.append(smooth(1, where[1]))
-    for copy in far_copies:
+    for sub in range(subs):
+        send(1, sub)
+    for copy in far_copies + outer_copies:
         copy.wait_recv()
+    unpack()
 
     @pl.when(tile == 0)
     def _():
@@ -204,23 +241,25 @@
         clear(past)
 
     outs.append(smooth(2, where[2]))
-
-    def loc_copies(g, sub, row0):
-        part = loc.at[
-            pl.ds(pl.multiple_of(row0, GROUP), GROUP),
-            pl.ds(pl.multiple_of(home * block + sub * WIDTH, WIDTH), WIDTH),
+    for sub in range(subs):
+        send(2, sub)
+
+    def loc_part(g, sub, owner):
+        return loc.at[
+            pl.ds(pl.multiple_of(where[g], GROUP), GROUP),
+            pl.ds(pl.multiple_of(owner * block + sub * PART, PART), PART),
         ]
-        return [
-            pltpu.make_async_remote_copy(
-                src_ref=part,
-                dst_ref=part,
-                send_sem=loc_send.at[g, sub, d - 1],
-                recv_sem=loc_recv.at[g, sub, d - 1],
-                device_id=(tile, lax.rem(home + d, groups)),
-                device_id_type=MESH,
-            )
-            for d in range(1, groups)
-        ]
+
+    def own_copy(g, sub, d):
+        part = loc_part(g, sub, home)
+        return pltpu.make_async_remote_copy(
+            src_ref=part,
+            dst_ref=part,
+            send_sem=loc_send.at[g, sub, d - 1],
+            recv_sem=loc_recv.at[g, sub, d - 1],
+            device_id=(tile, lax.rem(home + d, groups)),
+            device_id_type=MESH,
+        )
 
     def tukey(g, sub, row0):
         for n in range(sub * groups, (sub + 1) * groups):
@@ -230,8 +269,8 @@
                 z_copy(g, n, row0, local=True).wait()
 
         def cell_step(n, carry):
-            r = row0 + 8 * (n // (WIDTH // 128))
-            c = sub * WIDTH + 128 * lax.rem(n, WIDTH // 128)
+            r = row0 + 8 * (n // (PART // 128))
+            c = sub * PART + 128 * lax.rem(n, PART // 128)
             field = cells[:, :, pl.ds(pl.multiple_of(r, 8), 8), pl.ds(pl.multiple_of(c, 128), 128)]
             field = field.reshape(groups * seasons, 8, 128)
             number = groups * seasons
@@ -246,42 +285,77 @@
             loc[pl.ds(pl.multiple_of(r, 8), 8), pl.ds(pl.multiple_of(home * block + c, 128), 128)] = centre
             return carry
 
-        lax.fori_loop(0, (GROUP // 8) * (WIDTH // 128), cell_step, 0)
-        for copy in loc_copies(g, sub, row0):
-            copy.start()
-
+        lax.fori_loop(0, (GROUP // 8) * (PART // 128), cell_step, 0)
+        for d in range(1, groups):
+            own_copy(g, sub, d).start()
+
+    for g, sub in chunks:
+        tukey(g, sub, where[g])
+    own = pltpu.make_async_copy(
+        loc.at[:, pl.ds(pl.multiple_of(home * block, block), block)], own_out, out_sem.at[6]
+    )
+    own.start()
+    outs.append(own)
     for g in range(3):
         for sub in range(subs):
-            tukey(g, sub, where[g])
-    own = pltpu.make_async_copy(
-        loc.at[:, pl.ds(pl.multiple_of(home * block, block), block)], own_out, out_sem.at[3]
-    )
-    own.start()
-    for g in range(3):
-        for sub in range(subs):
-            for copy in loc_copies(g, sub, where[g]):
-                copy.wait_recv()
-    whole = pltpu.make_async_copy(loc, loc_out, out_sem.at[4])
-    whole.start()
-
-    for copy in near_copies + far_copies:
+            for d in range(1, groups):
+                own_copy(g, sub, d).wait_recv()
+        at = (pl.ds(pl.multiple_of(where[g], GROUP), GROUP), slice(None))
+        copy = pltpu.make_async_copy(loc.at[at], loc_out.at[at], out_sem.at[3 + g])
+        copy.start()
+        outs.append(copy)
+
+    for copy in near_copies + far_copies + outer_copies:
         copy.wait_send()
     for g in range(3):
         for n in range(subs * groups):
             if (n + 1) % groups:
                 z_copy(g, n, where[g]).wait_send()
-        for sub in range(subs):
-            for copy in loc_copies(g, sub, where[g]):
-                copy.wait_send()
-    for copy in outs + [own, whole]:
+    for chunk in chunks:
+        for d in range(1, groups):
+            own_copy(*chunk, d).wait_send()
+    for copy in outs:
         copy.wait()
+
+
+def finish_kernel(z_ref, loc_ref, own_ref, out_ref, own_out, buf, sems):
+    seasons = z_ref.shape[0]
+    copies = [pltpu.make_async_copy(own_ref, own_out, sems.at[seasons])]
+    copies[0].start()
+    for s in range(seasons):
+        buf[s] = z_ref[s] - loc_ref[...]
+        copy = pltpu.make_async_copy(buf.at[s], out_ref.at[s], sems.at[s])
+        copy.start()
+        copies.append(copy)
+    for copy in copies:
+        copy.wait()
+
+
+def finish(field, loc, own):
+    vmem = pl.BlockSpec(memory_space=pltpu.VMEM)
+    anywhere = pl.BlockSpec(memory_space=pl.ANY)
+    return pl.pallas_call(
+        finish_kernel,
+        out_shape=(
+            jax.ShapeDtypeStruct(field.shape, F32),
+            jax.ShapeDtypeStruct(own.shape, F32),
+        ),
+        in_specs=[vmem, vmem, anywhere],
+        out_specs=(anywhere,) * 2,
+        scratch_shapes=[
+            pltpu.VMEM(field.shape, F32),
+            pltpu.SemaphoreType.DMA((field.shape[0] + 1,)),
+        ],
+        compiler_params=pltpu.CompilerParams(vmem_limit_bytes=16 << 20),
+        name="anomalies",
+    )(field, loc, own)
 
 
 def on_device(yields, quality):
     seasons, rows, cols = yields.shape
     tiles, groups = lax.axis_size("tiles"), lax.axis_size("season")
     block = cols // groups
-    subs = block // WIDTH
+    subs = block // PART
     dma = pltpu.SemaphoreType.DMA
     anywhere = pl.BlockSpec(memory_space=pl.ANY)
     field, loc, own = pl.pallas_call(
@@ -296,6 +370,7 @@
         scratch_shapes=[
             pltpu.VMEM((seasons, rows + 2 * GROUP, cols), F32),
             pltpu.VMEM((seasons, rows + 2 * GROUP, cols), F32),
+            pltpu.VMEM((2, seasons - 1, 8, cols), F32),
             pltpu.VMEM((6 * GROUP * seasons, cols + 256), BF16),
             pltpu.VMEM((seasons, rows, cols), F32),
             pltpu.VMEM((groups, seasons, rows, block), F32),
@@ -308,19 +383,21 @@
             dma((2,)),
             dma((2,)),
             dma((2,)),
+            dma((2,)),
+            dma((2,)),
             dma((3, subs * groups)),
             dma((3, subs * groups)),
             dma((3, subs)),
             dma((3, subs, groups - 1)),
             dma((3, subs, groups - 1)),
-            dma((5,)),
+            dma((7,)),
         ],
         compiler_params=pltpu.CompilerParams(
             collective_id=0, has_side_effects=True, vmem_limit_bytes=48 << 20
         ),
         name="field_and_location",
     )(yields, quality)
-    return field - loc, own
+    return finish(field, loc, own)
 
 
 def solution(mesh):

time: 138 us -> 134 us (0.971)
  other arithmetic: 2.06 us -> 0 us
    pallas_call x1, Pallas kernels: 134 us -> 131 us  [on_device(): pl.pallas_call(functools.partial(kernel, tiles, groups), out_shape=(jax.S...]
    sub x1 -> x0, other arithmetic: 2.06 us -> none  [on_device(): return (field - loc, own)]
    pallas_call x0 -> x1, Pallas kernels: none -> 1.78 us  [finish(): pl.pallas_call(finish_kernel, out_shape=(jax.ShapeDtypeStruct(field.shape...]
where the time goes in v2:
time: 134 us
  Pallas kernels  133 us (99%)
    pallas_call x1, Pallas kernels, on_device(): pl.pallas_call(functools.partial(kernel, tiles, groups), out_shape=(jax.S...  131 us

profile of v2, /device:TPU:10, one launch (start us, length us, event | category | flops | bytes accessed | tf_op | source)
XLA Modules:
  0.0 133.7 jit_solution(17560369099536869218)
XLA Ops:
  0.6 131.2 %field_and_location.1 = (f32[8,48,2048]{2,1,0:T(8,128)S(1)}, f32[48,2048]{1,0:T(8,128)S(1)}, f32[48,512]{1,0:T(8,128)S(1)}) custom-call(f32[8,48,2048]{2,1,0:T(8,128)} %y_ref.1, f32[8,48,2048]{2,1,0:T(8,128)} %q_ref.1), custom_call_target="tpu_custom_call" | custom-call | tf_op jit(solution)/shard_map/field_and_location/pallas_call | solution.py:361
  131.9 1.8 %anomalies.1 = (f32[8,48,2048]{2,1,0:T(8,128)}, f32[48,512]{1,0:T(8,128)}) custom-call(f32[8,48,2048]{2,1,0:T(8,128)S(1)} %get-tuple-element.5.z_ref, f32[48,2048]{1,0:T(8,128)S(1)} %get-tuple-element.6.loc_ref, f32[48,512]{1,0:T(8,128)S(1)} %get-tuple-element.7.own_ref), custom_call_target="tpu_custom_call" | custom-call | tf_op jit(solution)/shard_map/anomalies/pallas_call | solution.py:337

commit v3 on v2

--- a/solution.py
+++ b/solution.py
@@ -244,17 +244,11 @@
     for sub in range(subs):
         send(2, sub)
 
-    def loc_part(g, sub, owner):
-        return loc.at[
-            pl.ds(pl.multiple_of(where[g], GROUP), GROUP),
-            pl.ds(pl.multiple_of(owner * block + sub * PART, PART), PART),
-        ]
-
     def own_copy(g, sub, d):
-        part = loc_part(g, sub, home)
+        here = pl.ds(pl.multiple_of(where[g], GROUP), GROUP)
         return pltpu.make_async_remote_copy(
-            src_ref=part,
-            dst_ref=part,
+            src_ref=loc.at[here, pl.ds(sub * PART, PART)],
+            dst_ref=loc_out.at[here, pl.ds(pl.multiple_of(home * block + sub * PART, PART), PART)],
             send_sem=loc_send.at[g, sub, d - 1],
             recv_sem=loc_recv.at[g, sub, d - 1],
             device_id=(tile, lax.rem(home + d, groups)),
@@ -282,7 +276,7 @@
                 root = jnp.maximum(1.0 - square * (1.0 / spread), 0.0)
                 weight = root * root
                 centre = centre + jnp.sum(weight * resid, axis=0) / (jnp.sum(weight, axis=0) + 1.0)
-            loc[pl.ds(pl.multiple_of(r, 8), 8), pl.ds(pl.multiple_of(home * block + c, 128), 128)] = centre
+            loc[pl.ds(pl.multiple_of(r, 8), 8), pl.ds(pl.multiple_of(c, 128), 128)] = centre
             return carry
 
         lax.fori_loop(0, (GROUP // 8) * (PART // 128), cell_step, 0)
@@ -291,19 +285,15 @@
 
     for g, sub in chunks:
         tukey(g, sub, where[g])
-    own = pltpu.make_async_copy(
-        loc.at[:, pl.ds(pl.multiple_of(home * block, block), block)], own_out, out_sem.at[6]
-    )
-    own.start()
-    outs.append(own)
+    mine = loc_out.at[:, pl.ds(pl.multiple_of(home * block, block), block)]
+    for i, target in enumerate((own_out, mine)):
+        copy = pltpu.make_async_copy(loc, target, out_sem.at[3 + i])
+        copy.start()
+        outs.append(copy)
     for g in range(3):
         for sub in range(subs):
             for d in range(1, groups):
                 own_copy(g, sub, d).wait_recv()
-        at = (pl.ds(pl.multiple_of(where[g], GROUP), GROUP), slice(None))
-        copy = pltpu.make_async_copy(loc.at[at], loc_out.at[at], out_sem.at[3 + g])
-        copy.start()
-        outs.append(copy)
 
     for copy in near_copies + far_copies + outer_copies:
         copy.wait_send()
@@ -374,7 +364,7 @@
             pltpu.VMEM((6 * GROUP * seasons, cols + 256), BF16),
             pltpu.VMEM((seasons, rows, cols), F32),
             pltpu.VMEM((groups, seasons, rows, block), F32),
-            pltpu.VMEM((rows, cols), F32),
+            pltpu.VMEM((rows, block), F32),
             pltpu.VMEM((6 * GROUP, 3 * WINDOW), BF16),
             pltpu.VMEM((SPAN, WIDTH), BF16),
             pltpu.VMEM((SPAN, WIDTH), BF16),
@@ -390,7 +380,7 @@
             dma((3, subs)),
             dma((3, subs, groups - 1)),
             dma((3, subs, groups - 1)),
-            dma((7,)),
+            dma((5,)),
         ],
         compiler_params=pltpu.CompilerParams(
             collective_id=0, has_side_effects=True, vmem_limit_bytes=48 << 20

time: 134 us -> 134 us (level)
  no operation moved by 1% of the time
where the time goes in v3:
time: 134 us
  Pallas kernels  133 us (99%)
    pallas_call x1, Pallas kernels, on_device(): pl.pallas_call(functools.partial(kernel, tiles, groups), out_shape=(jax.S...  131 us

profile of v3, /device:TPU:10, one launch (start us, length us, event | category | flops | bytes accessed | tf_op | source)
XLA Modules:
  0.0 133.5 jit_solution(18436682830048186479)
XLA Ops:
  0.6 131.1 %field_and_location.1 = (f32[8,48,2048]{2,1,0:T(8,128)S(1)}, f32[48,2048]{1,0:T(8,128)S(1)}, f32[48,512]{1,0:T(8,128)S(1)}) custom-call(f32[8,48,2048]{2,1,0:T(8,128)} %y_ref.1, f32[8,48,2048]{2,1,0:T(8,128)} %q_ref.1), custom_call_target="tpu_custom_call" | custom-call | tf_op jit(solution)/shard_map/field_and_location/pallas_call | solution.py:351
  131.7 1.8 %anomalies.1 = (f32[8,48,2048]{2,1,0:T(8,128)}, f32[48,512]{1,0:T(8,128)}) custom-call(f32[8,48,2048]{2,1,0:T(8,128)S(1)} %get-tuple-element.5.z_ref, f32[48,2048]{1,0:T(8,128)S(1)} %get-tuple-element.6.loc_ref, f32[48,512]{1,0:T(8,128)S(1)} %get-tuple-element.7.own_ref), custom_call_target="tpu_custom_call" | custom-call | tf_op jit(solution)/shard_map/anomalies/pallas_call | solution.py:327
